TPU v7x, 128 devices: a whole 4x4x4 slice. The times are simulated.
128 devices in a mesh: dp: 32 (over x_hi, y, z), tensor: 4 (over x_lo, core).
Axes of the slice: x: 4 (x_hi: 2, x_lo: 2; x = x_hi * 2 + x_lo), y: 4, z: 4, core: 2. Of those that a mesh axis runs over, the one named last changes fastest.
Arguments:
- hidden_in: bfloat16 [32768, 1536], P(('dp', 'tensor')), may hold values from -6 to 6
- cotangent: bfloat16 [32768, 1536], P(('dp', 'tensor')), may hold values from -6 to 6
- norm_gain: float32 [1536], replicated, may hold values from 0.1 to 1.9
- w_z: bfloat16 [1536, 3072], P('dp', 'tensor'), may hold values from -0.15625 to 0.15625
- w_x: bfloat16 [1536, 3072], P('dp', 'tensor'), may hold values from -0.15625 to 0.15625
- w_bc: bfloat16 [1536, 256], P('dp'), may hold values from -0.15625 to 0.15625
- w_dt: bfloat16 [1536, 48], P('dp', 'tensor'), may hold values from -0.15625 to 0.15625
- conv_x: float32 [5, 3072], P(None, 'tensor'), may hold values from -3 to 3
- conv_bc: float32 [5, 256], replicated, may hold values from -3 to 3
- head_params: float32 [3, 48], P(None, 'tensor'), may hold values from -7 to 3, as said below
- gate_gain: float32 [3072], P('tensor'), may hold values from 0.1 to 1.9
- w_out: bfloat16 [3072, 1536], P('tensor', 'dp'), may hold values from -0.109375 to 0.109375
Outputs:
- output: bfloat16 [32768, 1536], P(('dp', 'tensor'))
- input_grad: float32 [32768, 1536], P(('dp', 'tensor'))
- grad_norm_gain: float32 [1536], replicated
- grad_w_z: float32 [1536, 3072], P('dp', 'tensor')
- grad_w_x: float32 [1536, 3072], P('dp', 'tensor')
- grad_w_bc: float32 [1536, 256], P('dp')
- grad_w_dt: float32 [1536, 48], P('dp', 'tensor')
- grad_conv_x: float32 [5, 3072], P(None, 'tensor')
- grad_conv_bc: float32 [5, 256], replicated
- grad_head: float32 [3, 48], P(None, 'tensor')
- grad_gate_gain: float32 [3072], P('tensor')
- grad_w_out: float32 [3072, 1536], P('tensor', 'dp')
Inputs may be any that keep to these rules, and one draw needn't show every extreme that they name: `head_params`: row 0 holds logarithms of the heads' decay rates, row 1 the step-size biases, row 2 the skip weights.
All inputs are finite; a program needn't handle non-finite values.
Results may differ from a plain program's by a relative error of at most 0.0081.
Values may be sent and summed in bfloat16 or wider, within the bound.
No kernel may reach another device: no remote copies, remote signals or barrier semaphores. Data moves between devices by JAX's collectives and lax.ppermute only.
A program may use at most 128 MiB of HBM per device.

v0:
```python
import jax
import jax.numpy as jnp
from jax import lax
from jax.sharding import PartitionSpec as P

SPAN = 256


EPS = 1e-05


def causal_conv(values, kernel):
    tap_count = kernel.shape[0] - 1
    length = values.shape[0]
    padded = jnp.pad(values, ((tap_count - 1, 0), (0, 0)))
    result = kernel[tap_count] + padded[0:length] * kernel[0]
    for offset in range(1, tap_count):
        result = result + padded[offset : offset + length] * kernel[offset]
    return result


def state_scan(inputs, steps_dt, rates, b_rows, c_rows):
    length = inputs.shape[0]
    head_count = steps_dt.shape[1]
    head_width = inputs.shape[1] // head_count
    state_width = b_rows.shape[1]
    block_count = length // SPAN
    x_blocks = inputs.reshape(block_count, SPAN, head_count, head_width)
    dt_blocks = steps_dt.reshape(block_count, SPAN, head_count)
    b_blocks = b_rows.reshape(block_count, SPAN, state_width)
    c_blocks = c_rows.reshape(block_count, SPAN, state_width)
    row_index = jnp.arange(SPAN)
    mask_3d = (row_index[:, None] >= row_index[None, :])[:, :, None]

    def one_block(carried, pieces):
        x_part, dt_part, b_part, c_part = pieces
        log_decay = jnp.cumsum(dt_part * rates, axis=0)
        spread = log_decay[:, None, :] - log_decay[None, :, :]
        decays = jnp.where(mask_3d, jnp.exp(jnp.where(mask_3d, spread, 0.0)), 0.0)
        scores = jnp.einsum("in,jn->ij", c_part, b_part, precision=lax.Precision.HIGHEST)
        weights = decays * scores[:, :, None] * dt_part[None, :, :]
        inside = jnp.einsum("ijh,jhp->ihp", weights, x_part, precision=lax.Precision.HIGHEST)
        carried_out = (
            jnp.einsum("in,hnp->ihp", c_part, carried, precision=lax.Precision.HIGHEST)
            * jnp.exp(log_decay)[:, :, None]
        )
        to_end = jnp.exp(log_decay[-1][None, :] - log_decay) * dt_part
        added_state = jnp.einsum(
            "jn,jhp->hnp", b_part, x_part * to_end[:, :, None], precision=lax.Precision.HIGHEST
        )
        updated = carried * jnp.exp(log_decay[-1])[:, None, None] + added_state
        return (updated, inside + carried_out)

    initial = jnp.zeros((head_count, state_width, head_width), jnp.float32)
    last_state, y_blocks = lax.scan(
        jax.checkpoint(one_block), initial, (x_blocks, dt_blocks, b_blocks, c_blocks)
    )
    return y_blocks.reshape(length, head_count * head_width)


def mixer_core(gate_pre, x_pre, bc_pre, dt_pre, conv_x, conv_bc, head_params):
    x_conv = jax.nn.silu(causal_conv(x_pre, conv_x))
    bc_conv = jax.nn.silu(causal_conv(bc_pre, conv_bc))
    state_width = bc_conv.shape[1] // 2
    steps_dt = jax.nn.softplus(dt_pre + head_params[1])
    rates = -jnp.exp(head_params[0])
    scanned = state_scan(
        x_conv, steps_dt, rates, bc_conv[:, :state_width], bc_conv[:, state_width:]
    )
    head_count = steps_dt.shape[1]
    length = x_conv.shape[0]
    skipped = (x_conv.reshape(length, head_count, -1) * head_params[2][None, :, None]).reshape(
        length, -1
    )
    return (scanned + skipped) * jax.nn.silu(gate_pre)


def contract(left, right, left_dim, right_dim):
    return lax.dot_general(
        left, right, (((left_dim,), (right_dim,)), ((), ())), preferred_element_type=jnp.float32
    )


def on_device(
    hidden_in,
    cotangent,
    norm_gain,
    w_z,
    w_x,
    w_bc,
    w_dt,
    conv_x,
    conv_bc,
    head_params,
    gate_gain,
    w_out,
):

    def fetch_inputs():
        return (
            lax.all_gather(w_z, "dp", axis=0, tiled=True),
            lax.all_gather(w_x, "dp", axis=0, tiled=True),
            lax.all_gather(w_bc, "dp", axis=0, tiled=True),
            lax.all_gather(w_dt, "dp", axis=0, tiled=True),
        )

    def fetch_output():
        return lax.all_gather(w_out, "dp", axis=1, tiled=True)

    resid = hidden_in.astype(jnp.float32)
    inv_rms = lax.rsqrt(jnp.mean(resid * resid, axis=1, keepdims=True) + EPS)
    normed = (resid * inv_rms * norm_gain).astype(jnp.bfloat16)
    tokens_all = lax.all_gather(normed, "tensor", axis=0, tiled=True)
    full_z, full_x, full_bc, full_dt = fetch_inputs()
    gate_pre = jnp.dot(tokens_all, full_z, preferred_element_type=jnp.float32)
    x_pre = jnp.dot(tokens_all, full_x, preferred_element_type=jnp.float32)
    bc_pre = jnp.dot(tokens_all, full_bc, preferred_element_type=jnp.float32)
    dt_pre = jnp.dot(tokens_all, full_dt, preferred_element_type=jnp.float32)
    gated, mixer_back = jax.vjp(
        mixer_core, gate_pre, x_pre, bc_pre, dt_pre, conv_x, conv_bc, head_params
    )
    width_all = gated.shape[1] * lax.axis_size("tensor")
    squares = lax.psum(jnp.sum(gated * gated, axis=1), "tensor")
    gate_rms = lax.rsqrt(squares / width_all + EPS)[:, None]
    normed_y = (gated * gate_rms * gate_gain).astype(jnp.bfloat16)
    full_out = fetch_output()
    partial_out = jnp.dot(normed_y, full_out, preferred_element_type=jnp.float32)
    mixed = lax.psum_scatter(partial_out, "tensor", scatter_dimension=0, tiled=True)
    output = (resid + mixed).astype(jnp.bfloat16)
    cot_all = lax.all_gather(cotangent, "tensor", axis=0, tiled=True)
    grad_out_full = contract(normed_y, cot_all, 0, 0)
    back_out = fetch_output()
    back_z, back_x, back_bc, back_dt = fetch_inputs()
    d_normed_y = contract(cot_all, back_out, 1, 1)
    scaled = d_normed_y * gate_gain
    grad_gate_part = jnp.sum(d_normed_y * gated * gate_rms, axis=0)
    inner = lax.psum(jnp.sum(gated * scaled, axis=1), "tensor")[:, None]
    d_gated = gate_rms * scaled - gated * (gate_rms * gate_rms * gate_rms) * inner / width_all
    d_gate, d_x, d_bc_part, d_dt, grad_conv_x_part, grad_conv_bc_part, grad_head_part = mixer_back(
        d_gated
    )
    d_bc, grad_conv_bc_group = lax.psum((d_bc_part, grad_conv_bc_part), "tensor")
    gate_low = d_gate.astype(jnp.bfloat16)
    x_low = d_x.astype(jnp.bfloat16)
    bc_low = d_bc.astype(jnp.bfloat16)
    dt_low = d_dt.astype(jnp.bfloat16)
    partial_in = (
        contract(gate_low, back_z, 1, 1)
        + contract(x_low, back_x, 1, 1)
        + contract(dt_low, back_dt, 1, 1)
    )
    d_normed = lax.psum_scatter(partial_in, "tensor", scatter_dimension=0, tiled=True)
    row_count = hidden_in.shape[0]
    own_bc = lax.dynamic_slice_in_dim(bc_low, lax.axis_index("tensor") * row_count, row_count, 0)
    d_normed = d_normed + contract(own_bc, back_bc, 1, 1)
    grad_gain_part = jnp.sum(d_normed * resid * inv_rms, axis=0)
    d_scaled = d_normed * norm_gain
    cubed = inv_rms * inv_rms * inv_rms
    input_grad = (
        inv_rms * d_scaled
        - resid * cubed * jnp.sum(resid * d_scaled, axis=1, keepdims=True) / resid.shape[1]
        + cotangent.astype(jnp.float32)
    )
    grad_norm_gain = lax.psum(grad_gain_part, ("dp", "tensor"))
    grad_z_full = contract(tokens_all, gate_low, 0, 0)
    grad_x_full = contract(tokens_all, x_low, 0, 0)
    grad_bc_full = contract(tokens_all, bc_low, 0, 0)
    grad_dt_full = contract(tokens_all, dt_low, 0, 0)
    grad_w_z, grad_w_x, grad_w_bc, grad_w_dt = (
        lax.psum_scatter(grad_z_full, "dp", scatter_dimension=0, tiled=True),
        lax.psum_scatter(grad_x_full, "dp", scatter_dimension=0, tiled=True),
        lax.psum_scatter(grad_bc_full, "dp", scatter_dimension=0, tiled=True),
        lax.psum_scatter(grad_dt_full, "dp", scatter_dimension=0, tiled=True),
    )
    grad_w_out = lax.psum_scatter(grad_out_full, "dp", scatter_dimension=1, tiled=True)
    grad_conv_x, grad_head, grad_gate_gain, grad_conv_bc = lax.psum(
        (grad_conv_x_part, grad_head_part, grad_gate_part, grad_conv_bc_group), "dp"
    )
    return (
        output,
        input_grad,
        grad_norm_gain,
        grad_w_z,
        grad_w_x,
        grad_w_bc,
        grad_w_dt,
        grad_conv_x,
        grad_conv_bc,
        grad_head,
        grad_gate_gain,
        grad_w_out,
    )


def solution(mesh):
    placed = (
        P(("dp", "tensor"), None),
        P(("dp", "tensor"), None),
        P(),
        P("dp", "tensor"),
        P("dp", "tensor"),
        P("dp", None),
        P("dp", "tensor"),
        P(None, "tensor"),
        P(),
        P(None, "tensor"),
        P("tensor"),
        P("tensor", "dp"),
    )
    return jax.shard_map(
        on_device,
        mesh=mesh,
        in_specs=placed,
        out_specs=(
            P(("dp", "tensor"), None),
            P(("dp", "tensor"), None),
            P(),
            P("dp", "tensor"),
            P("dp", "tensor"),
            P("dp", None),
            P("dp", "tensor"),
            P(None, "tensor"),
            P(),
            P(None, "tensor"),
            P("tensor"),
            P("tensor", "dp"),
        ),
        check_vma=False,
    )
```

profile of v0, /device:TPU:1, one launch (start us, length us, event | category | flops | bytes accessed | tf_op | source)
XLA Modules:
  0.0 1925.2 jit_solution(6014565604340860553)
XLA Ops:
  18.1 84.1 %all-gather = bf16[32,48,12]{1,2,0:T(8,128)(2,1)S(1)} all-gather(bf16[1,48,12]{1,2,0:T(8,128)(2,1)S(1)} %bitcast.412), channel_id=1, replica_groups=mesh['dp'=32,'tensor'=4] {'dp'}, dimensions={0}, use_global_device_ids=true | all-gather | bytes 38016 | tf_op jit(solution)/shard_map/all_gather | solution.py:104
  103.0 84.3 %all_gather.29 = bf16[1536,256]{1,0:T(8,128)(2,1)} all-gather(bf16[48,256]{1,0:T(8,128)(2,1)S(1)} %copy-done.24), channel_id=1, replica_groups=mesh['dp'=32,'tensor'=4] {'dp'}, dimensions={0}, use_global_device_ids=true | all-gather | bytes 811008 | tf_op jit(solution)/shard_map/all_gather | solution.py:103
  187.2 3.7 compare_select_fusion.2
  199.7 4.3 fusion.143
  204.0 4.2 fusion.103
  210.6 2.9 reshape.315
  213.5 4.3 copy.150
  220.1 126.1 %while.44 = (s32[]{:T(128)}, f32[12,128,64]{1,2,0:T(8,128)S(1)}, f32[4,256,12,64]{1,0,3,2:T(4,128)}, f32[4,12,128,64]{2,3,1,0:T(8,128)}, f32[4,256,12]{1,2,0:T(8...) while((s32[]{:T(128)}, f32[12,128,64]{1,2,0:T(8,128)S(1)}, ...), condition=%wide.region_4.5_spmd.clone.clone, body=%wide.region_1.4_spmd.clone.clone.sunk | while | flops 1313842176 | bytes 10902735 | solution.py:55
  227.9 5.0 fusion.265
  233.7 17.9 dynamic_update_slice.74
  259.4 5.0 fusion.265
  265.3 17.9 dynamic_update_slice.74
  291.0 5.0 fusion.265
  296.8 17.9 dynamic_update_slice.74
  322.5 5.0 fusion.265
  328.3 17.9 dynamic_update_slice.74
  346.2 4.3 copy.216
  350.5 3.7 copy.152
  354.2 8.7 multiply_reduce_fusion.11
  362.9 47.3 %psum.63 = f32[1024]{0:T(1024)S(1)} all-reduce(f32[1024]{0:T(1024)} %get-tuple-element.798), channel_id=1, replica_groups=mesh['dp'=32,'tensor'=4] {'tensor'}, use_global_device_ids=true, to_apply=%region_6.7 | all-reduce | flops 1024 | bytes 8192 | tf_op jit(solution)/shard_map/psum | solution.py:123
  410.8 8.7 multiply_reduce_fusion.4
  419.5 6.3 psum.64
  425.8 8.5 multiply_reduce_fusion.5
  436.7 2.9 reshape.319
  444.3 199.9 %while.43 = (s32[]{:T(128)}, f32[12]{0:T(128)}, f32[12,128,64]{1,2,0:T(8,128)S(1)}, f32[4,256,12,64]{1,0,3,2:T(4,128)}, f32[4,256,12]{1,0,2:T(4,128)}, /*index=5...) while((s32[]{:T(128)}, f32[12]{0:T(128)}, ...), condition=%wide.region_24.25_spmd.clone, body=%wide.region_10.24_spmd.clone.sunk | while | flops 3038789632 | bytes 27654896 | solution.py:55
  447.1 2.7 constant_dynamic-slice_fusion.2
  453.5 5.0 fusion.245
  461.9 2.9 fusion.251
  465.8 2.5 reduce-window.74
  475.9 17.8 dynamic_update_slice.71
  496.5 2.7 constant_dynamic-slice_fusion.2
  502.9 5.0 fusion.245
  511.3 2.9 fusion.251
  515.2 2.5 reduce-window.74
  525.9 17.8 dynamic_update_slice.71
  546.5 2.7 constant_dynamic-slice_fusion.2
  552.9 5.0 fusion.245
  561.3 2.9 fusion.251
  565.2 2.5 reduce-window.74
  575.9 17.8 dynamic_update_slice.71
  596.6 2.7 constant_dynamic-slice_fusion.2
  603.0 5.0 fusion.245
  611.4 2.9 fusion.251
  626.0 17.8 dynamic_update_slice.71
  646.1 3.9 fusion.124
  652.5 3.8 copy.158
  656.3 8.7 multiply_reduce_fusion.9
  668.6 2.6 fusion.145
  671.3 2.6 fusion.146
  674.0 3.6 add_add_fusion
  679.4 6.3 fusion.131
  690.2 28.7 %all-reduce.30 = (bf16[1024,256]{1,0:T(8,128)(2,1)}, f32[5,256]{1,0:T(8,128)S(1)}) all-reduce(f32[1024,256]{1,0:T(8,128)} %pad_add_fusion.3, f32[5,256]{1,0:T(8,128)S(1)} %pad_add_fusion.7), channel_id=1, replica_groups=mesh['dp'=32,'tensor'=4] {'tensor'}, use_global_device_ids=true, to_apply=%region_26.27 | all-reduce | flops 263424 | bytes 1583104 | tf_op jit(solution)/shard_map/psum | solution.py:142
  718.9 3.2 fusion.149
  722.2 7.9 fusion.130
  730.1 5.7 fusion.147
  736.0 5.8 fusion.148
  743.4 151.0 %all-reduce.27 = (f32[5,768]{1,0:T(8,128)}, f32[5,256]{1,0:T(8,128)}, f32[3,12]{1,0:T(4,128)}, f32[768]{0:T(1024)}) all-reduce(f32[5,768]{1,0:T(8,128)S(1)} %pad_add_fusion.6, f32[5,256]{1,0:T(8,128)S(1)} %get-tuple-element.785, f32[3,12]{1,0:T(4,128)S(1)} %pad_add_fusion.8, ...), channel_id=1, replica_groups=mesh['dp'=32,'tensor'=4] {'dp'}, use_global_device_ids=true, to_apply=%region_39.40 | all-reduce | flops 5924 | bytes 47392 | tf_op jit(solution)/shard_map/psum | solution.py:176
  895.8 34.5 %reduce-scatter.12.cloned.1.call-done = f32[256,1536]{1,0:T(8,128)} async-done(((f32[1024,1536]{1,0:T(8,128)}), f32[256,1536]{1,0:T(8,128)}) %reduce-scatter.12.cloned.1.call-update) | async-done | bytes 1572880 | tf_op jit(solution)/shard_map/reduce_scatter | solution.py:152
  932.7 65.8 %psum.66 = f32[1536]{0:T(1024)} all-reduce(f32[1536]{0:T(1024)S(1)} %get-tuple-element.720), channel_id=1, replica_groups=mesh['dp'=32,'tensor'=4] {'dp','tensor'}, use_global_device_ids=true, to_apply=%region_29.30 | all-reduce | flops 1536 | bytes 12288 | tf_op jit(solution)/shard_map/psum | solution.py:164
  998.5 3.3 fusion.111
  1001.8 221.6 %reduce-scatter.18.cloned.1.call-done = f32[48,256]{1,0:T(8,128)} async-done(((f32[1536,256]{1,0:T(8,128)}), f32[48,256]{1,0:T(8,128)}) %reduce-scatter.18.cloned.1.call-update) | async-done | bytes 49168 | tf_op jit(solution)/shard_map/reduce_scatter | solution.py:172
  1223.4 231.6 %reduce-scatter.20.cloned.1.call-done = f32[768,48]{0,1:T(8,128)} async-done(((f32[768,1536]{0,1:T(8,128)}), f32[768,48]{0,1:T(8,128)}) %reduce-scatter.20.cloned.1.call-update) | async-done | bytes 147472 | tf_op jit(solution)/shard_map/reduce_scatter | solution.py:175
  1455.0 231.7 %reduce-scatter.14.cloned.1.call-done = f32[48,768]{1,0:T(8,128)} async-done(((f32[1536,768]{1,0:T(8,128)}), f32[48,768]{1,0:T(8,128)}) %reduce-scatter.14.cloned.1.call-update) | async-done | bytes 147472 | tf_op jit(solution)/shard_map/reduce_scatter | solution.py:170
  1686.7 231.5 %reduce-scatter.16.cloned.1.call-done = f32[48,768]{1,0:T(8,128)} async-done(((f32[1536,768]{1,0:T(8,128)}), f32[48,768]{1,0:T(8,128)}) %reduce-scatter.16.cloned.1.call-update) | async-done | bytes 147472 | tf_op jit(solution)/shard_map/reduce_scatter | solution.py:171
  (447 shorter events, 163.9 us)
Async XLA Ops:
  7.2 7.6 copy-start.47
  7.2 8.9 copy-start.46
  7.2 10.3 copy-start.32
  7.2 10.9 copy-start.43
  7.2 95.8 %copy-start.24 = (bf16[48,256]{1,0:T(8,128)(2,1)S(1)}, bf16[48,256]{1,0:T(8,128)(2,1)}, u32[]{:S(2)}) copy-start(bf16[48,256]{1,0:T(8,128)(2,1)} %param.21) | copy-start | bytes 73732
  7.2 180.0 %all-gather.7.cloned.1.call-start = ((), (), s32[]{:S(2)}) async-start(), calls=%async_computation.7 | async-start | bytes 3932160 | tf_op jit(solution)/shard_map/all_gather | solution.py:113
  9.3 0.6 copy-start.27
  12.1 187.6 %all-gather.9.cloned.1.call-start = ((), (), s32[]{:S(2)}) async-start(), calls=%async_computation.8 | async-start | bytes 2433024 | tf_op jit(solution)/shard_map/all_gather | solution.py:102
  12.9 341.3 %all-gather.11.cloned.1.call-start = ((), (), s32[]{:S(2)}) async-start(), calls=%async_computation.9 | async-start | bytes 2433024 | tf_op jit(solution)/shard_map/all_gather | solution.py:101
  13.6 397.2 %all-gather.13.cloned.1.call-start = ((), (), s32[]{:S(2)}) async-start(), calls=%async_computation.10 | async-start | bytes 2433024 | tf_op jit(solution)/shard_map/all_gather | solution.py:108
  14.2 396.6 %all-gather.15.cloned.1.call-start = ((), (), s32[]{:S(2)}) async-start(), calls=%async_computation.12 | async-start | bytes 3932160 | tf_op jit(solution)/shard_map/all_gather | solution.py:130
  14.8 879.6 %reduce-scatter.22.cloned.1.call-start = ((), (), s32[]{:S(2)}) async-start(), calls=%async_computation.18 | async-start | bytes 811008
  187.2 6.6 copy-start
  193.8 3.1 copy-start.33
  193.9 3.1 copy-start.35
  193.9 3.1 copy-start.37
  193.9 3.1 copy-start.39
  193.9 3.1 copy-start.42
  196.0 1.0 copy-start.9
  199.7 4.3 copy-start.21
  199.7 4.3 copy-start.26
  204.0 4.2 copy-start.7
  217.8 2.3 copy-start.8
  217.8 2.3 copy-start.20
  217.8 2.3 copy-start.25
  350.5 3.7 copy-start.1
  410.8 15.0 copy-start.3
  646.1 4.0 copy-start.5
  650.0 280.3 %reduce-scatter.12.cloned.1.call-start = ((), (), s32[]{:S(2)}) async-start(), calls=%async_computation.13 | async-start | bytes 7864320 | tf_op jit(solution)/shard_map/reduce_scatter | solution.py:152
  652.5 3.8 copy-start.4
  652.5 3.8 copy-start.23
  656.3 8.7 copy-start.22
  666.0 1.4 copy-start.17
  666.0 2.6 copy-start.49
  667.0 4.3 copy-start.16
  668.6 2.7 copy-start.48
  671.3 2.7 copy-start.18
  677.5 1.9 copy-start.13
  677.5 1.9 copy-start.30
  677.5 1.9 copy-start.45
  677.6 320.9 %reduce-scatter.10.cloned.1.call-start = ((), (), s32[]{:S(2)}) async-start(), calls=%async_computation.11 | async-start | bytes 7864320 | tf_op jit(solution)/shard_map/reduce_scatter | solution.py:128
  685.8 1.2 copy-start.10
  685.8 1.6 copy-start.11
  685.8 1.7 copy-start.14
  685.8 1.8 copy-start.15
  685.8 2.7 copy-start.34
  685.8 2.7 copy-start.36
  685.8 2.7 copy-start.38
  685.8 2.7 copy-start.40
  685.8 537.6 %reduce-scatter.18.cloned.1.call-start = ((), (), s32[]{:S(2)}) async-start(), calls=%async_computation.16 | async-start | bytes 1622016 | tf_op jit(solution)/shard_map/reduce_scatter | solution.py:172
  688.9 30.0 %copy-start.2 = (bf16[1024,1536]{1,0:T(8,128)(2,1)S(1)}, bf16[1024,1536]{1,0:T(8,128)(2,1)}, u32[]{:S(2)}) copy-start(bf16[1024,1536]{1,0:T(8,128)(2,1)} %all-gather.7.cloned.1.call-done) | copy-start | bytes 9437188
  722.1 732.9 %reduce-scatter.20.cloned.1.call-start = ((), (), s32[]{:S(2)}) async-start(), calls=%async_computation.17 | async-start | bytes 4866048 | tf_op jit(solution)/shard_map/reduce_scatter | solution.py:175
  730.1 956.6 %reduce-scatter.14.cloned.1.call-start = ((), (), s32[]{:S(2)}) async-start(), calls=%async_computation.14 | async-start | bytes 4866048 | tf_op jit(solution)/shard_map/reduce_scatter | solution.py:170
  735.9 1182.3 %reduce-scatter.16.cloned.1.call-start = ((), (), s32[]{:S(2)}) async-start(), calls=%async_computation.15 | async-start | bytes 4866048 | tf_op jit(solution)/shard_map/reduce_scatter | solution.py:171
  741.8 0.7 copy-start.29
  741.8 0.9 copy-start.31
  741.8 1.6 copy-start.44
  741.8 188.5 %copy-start.6 = (bf16[256,1536]{1,0:T(8,128)(2,1)S(1)}, bf16[256,1536]{1,0:T(8,128)(2,1)}, u32[]{:S(2)}) copy-start(bf16[256,1536]{1,0:T(8,128)(2,1)} %param.16) | copy-start | bytes 2359300
  741.8 188.5 %copy-start.19 = (f32[1536]{0:T(1024)S(1)}, f32[1536]{0:T(1024)}, u32[]{:S(2)}) copy-start(f32[1536]{0:T(1024)} %param.18) | copy-start | bytes 18436
  741.8 188.5 %copy-start.28 = (f32[256]{0:T(256)S(1)}, f32[256]{0:T(256)}, u32[]{:S(2)}) copy-start(f32[256]{0:T(256)} %copy-done.27) | copy-start | bytes 3076
  741.9 256.6 %copy-start.12 = (bf16[256,1536]{1,0:T(8,128)(2,1)S(1)}, bf16[256,1536]{1,0:T(8,128)(2,1)}, u32[]{:S(2)}) copy-start(bf16[256,1536]{1,0:T(8,128)(2,1)} %param.17) | copy-start | bytes 2359300
  741.9 256.6 %copy-start.41 = (f32[256]{0:T(256)S(1)}, f32[256]{0:T(256)}, u32[]{:S(2)}) copy-start(f32[256]{0:T(256)} %get-tuple-element.841) | copy-start | bytes 3076
Sparse Core Ops, SparseCore 0:
  12.2 41.9 all-gather.6
  57.2 70.3 all-gather.8
  130.6 70.7 all-gather.10
  204.3 70.1 all-gather.12
  276.0 38.4 all-gather.14
  650.1 215.2 reduce-scatter.21
  868.0 62.2 reduce-scatter.11
  932.8 64.0 reduce-scatter.9
  1003.1 220.2 reduce-scatter.17
  1228.9 226.0 reduce-scatter.19
  1460.7 225.9 reduce-scatter.13
  1692.2 225.9 reduce-scatter.15
where the time goes:
time: 1940 us; the launch traced here: 1930 us
  waiting for transfers between devices  953 us (49%)
  blocking collectives  467 us (24%)
  local copies, waits for them, and re-layouts  241 us (12%)
  matrix products  177 us (9%)
  other arithmetic  69.5 us (4%)
    reduce_scatter x1, waiting for transfers between devices, on_device(): lax.psum_scatter(grad_z_full, 'dp', scatter_dimension=0, tiled=True)  232 us
    reduce_scatter x1, waiting for transfers between devices, on_device(): lax.psum_scatter(grad_out_full, 'dp', scatter_dimension=1, tiled=True)  232 us
    reduce_scatter x1, waiting for transfers between devices, on_device(): lax.psum_scatter(grad_x_full, 'dp', scatter_dimension=0, tiled=True)  232 us
    reduce_scatter x1, waiting for transfers between devices, on_device(): lax.psum_scatter(grad_bc_full, 'dp', scatter_dimension=0, tiled=True)  222 us
    dynamic_update_slice x24, local copies, waits for them, and re-layouts, state_scan(): lax.scan(jax.checkpoint(one_block), initial, (x_blocks, dt_blocks, b_bloc...  155 us
    psum x1, blocking collectives, on_device(): lax.psum((grad_conv_x_part, grad_head_part, grad_gate_part, grad_conv_bc_...  151 us
    all_gather x1, blocking collectives, fetch_inputs(): lax.all_gather(w_bc, 'dp', axis=0, tiled=True)  84.3 us
    all_gather x1, blocking collectives, fetch_inputs(): lax.all_gather(w_dt, 'dp', axis=0, tiled=True)  84.1 us
  transfers between devices with their start and end apart: 12, of which 5 were waited for; matrix products, arithmetic and copies ran while one was open for 13% of the time, Pallas kernels for 0%

commit v1 on v0

v1 whole, which is shorter than its diff:
```python
import jax
import jax.numpy as jnp
from jax import lax
from jax.sharding import Mesh, PartitionSpec as P

SPAN = 256
EPS = 1e-05
AXES = ("xh", "y", "z", "xl", "core")
DP = ("xh", "y", "z")
TN = ("xl", "core")
BF = jnp.bfloat16
F32 = jnp.float32


def causal_conv(values, kernel):
    tap_count = kernel.shape[0] - 1
    length = values.shape[0]
    padded = jnp.pad(values, ((tap_count - 1, 0), (0, 0)))
    result = kernel[tap_count] + padded[0:length] * kernel[0]
    for offset in range(1, tap_count):
        result = result + padded[offset : offset + length] * kernel[offset]
    return result


def state_scan(inputs, steps_dt, rates, b_rows, c_rows):
    length = inputs.shape[0]
    head_count = steps_dt.shape[1]
    head_width = inputs.shape[1] // head_count
    state_width = b_rows.shape[1]
    block_count = length // SPAN
    x_blocks = inputs.reshape(block_count, SPAN, head_count, head_width)
    dt_blocks = steps_dt.reshape(block_count, SPAN, head_count)
    b_blocks = b_rows.reshape(block_count, SPAN, state_width)
    c_blocks = c_rows.reshape(block_count, SPAN, state_width)
    row_index = jnp.arange(SPAN)
    mask_3d = (row_index[:, None] >= row_index[None, :])[:, :, None]

    def one_block(carried, pieces):
        x_part, dt_part, b_part, c_part = pieces
        log_decay = jnp.cumsum(dt_part * rates, axis=0)
        spread = log_decay[:, None, :] - log_decay[None, :, :]
        decays = jnp.where(mask_3d, jnp.exp(jnp.where(mask_3d, spread, 0.0)), 0.0)
        scores = jnp.einsum("in,jn->ij", c_part, b_part, precision=lax.Precision.HIGHEST)
        weights = decays * scores[:, :, None] * dt_part[None, :, :]
        inside = jnp.einsum("ijh,jhp->ihp", weights, x_part, precision=lax.Precision.HIGHEST)
        carried_out = (
            jnp.einsum("in,hnp->ihp", c_part, carried, precision=lax.Precision.HIGHEST)
            * jnp.exp(log_decay)[:, :, None]
        )
        to_end = jnp.exp(log_decay[-1][None, :] - log_decay) * dt_part
        added_state = jnp.einsum(
            "jn,jhp->hnp", b_part, x_part * to_end[:, :, None], precision=lax.Precision.HIGHEST
        )
        updated = carried * jnp.exp(log_decay[-1])[:, None, None] + added_state
        return (updated, inside + carried_out)

    initial = jnp.zeros((head_count, state_width, head_width), F32)
    last_state, y_blocks = lax.scan(
        jax.checkpoint(one_block), initial, (x_blocks, dt_blocks, b_blocks, c_blocks)
    )
    return y_blocks.reshape(length, head_count * head_width)


def mixer_inner(x_pre, bc_pre, dt_pre, conv_x, conv_bc, head_params):
    x_conv = jax.nn.silu(causal_conv(x_pre, conv_x))
    bc_conv = jax.nn.silu(causal_conv(bc_pre, conv_bc))
    state_width = bc_conv.shape[1] // 2
    steps_dt = jax.nn.softplus(dt_pre + head_params[1])
    rates = -jnp.exp(head_params[0])
    scanned = state_scan(
        x_conv, steps_dt, rates, bc_conv[:, :state_width], bc_conv[:, state_width:]
    )
    head_count = steps_dt.shape[1]
    length = x_conv.shape[0]
    skipped = (x_conv.reshape(length, head_count, -1) * head_params[2][None, :, None]).reshape(
        length, -1
    )
    return scanned + skipped


def contract(left, right, left_dim, right_dim):
    return lax.dot_general(
        left, right, (((left_dim,), (right_dim,)), ((), ())), preferred_element_type=F32
    )


def swap(value, axis):
    return lax.ppermute(value, axis, [(0, 1), (1, 0)])


def gather_dp(shard):
    count = lax.axis_size(DP)
    spread = jnp.broadcast_to(shard[None], (count,) + shard.shape)
    got = lax.all_to_all(spread, DP, 0, 0, tiled=True)
    return got.reshape((count * shard.shape[0],) + shard.shape[1:])


def scatter_dp(partial):
    count = lax.axis_size(DP)
    got = lax.all_to_all(partial, DP, 0, 0, tiled=True)
    return got.reshape((count, -1) + partial.shape[1:]).astype(F32).sum(axis=0)


def gather_tn(own):
    far = swap(own, "xl")
    first = lax.axis_index("xl") == 0
    pair = jnp.stack([jnp.where(first, own, far), jnp.where(first, far, own)])
    other = swap(pair, "core")
    even = lax.axis_index("core") == 0
    both = jnp.stack([jnp.where(even, pair, other), jnp.where(even, other, pair)], axis=1)
    return both.reshape((-1,) + own.shape[1:])


def sum_tn(value):
    total = value
    for mask in (1, 2, 3):
        total = total + lax.ppermute(value, TN, [(i, i ^ mask) for i in range(4)])
    return total


def scatter_tn(partial):
    rows = partial.shape[0] // 4
    split = partial.reshape((2, 2, rows) + partial.shape[1:])
    core, xl = lax.axis_index("core"), lax.axis_index("xl")
    keep = lax.dynamic_index_in_dim(split, core, 1, keepdims=False)
    send = lax.dynamic_index_in_dim(split, 1 - core, 1, keepdims=False).astype(BF)
    half = keep + swap(send, "core").astype(F32)
    keep = lax.dynamic_index_in_dim(half, xl, 0, keepdims=False)
    send = lax.dynamic_index_in_dim(half, 1 - xl, 0, keepdims=False).astype(BF)
    return keep + swap(send, "xl").astype(F32)


def on_device(
    hidden_in,
    cotangent,
    norm_gain,
    w_z,
    w_x,
    w_bc,
    w_dt,
    conv_x,
    conv_bc,
    head_params,
    gate_gain,
    w_out,
):
    wide = w_x.shape[1]
    states = w_bc.shape[1]
    quarter = states // 4
    heads = w_dt.shape[1]
    rank = lax.axis_index(TN)

    first = jnp.concatenate([w_x, w_bc, w_dt], axis=1)
    full_first = gather_dp(first)
    second = jnp.concatenate([w_z, w_out.T], axis=1)
    full_second = gather_dp(second)
    full_x = full_first[:, :wide]
    full_bc = full_first[:, wide : wide + states]
    full_dt = full_first[:, wide + states :]
    full_z = full_second[:, :wide]
    full_out = full_second[:, wide:]
    tokens = gather_tn(hidden_in).astype(F32)
    cot_all = gather_tn(cotangent)

    resid = hidden_in.astype(F32)
    inv_rms = lax.rsqrt(jnp.mean(resid * resid, axis=1, keepdims=True) + EPS)
    inv_all = lax.rsqrt(jnp.mean(tokens * tokens, axis=1, keepdims=True) + EPS)
    normed = (tokens * inv_all * norm_gain).astype(BF)

    x_pre = jnp.dot(normed, full_x, preferred_element_type=F32)
    bc_pre = jnp.dot(normed, full_bc, preferred_element_type=F32)
    dt_pre = jnp.dot(normed, full_dt, preferred_element_type=F32)
    mixed, mixer_back = jax.vjp(
        mixer_inner, x_pre, bc_pre, dt_pre, conv_x, conv_bc, head_params
    )
    gate_pre = jnp.dot(normed, full_z, preferred_element_type=F32)
    gate_sig = jax.nn.sigmoid(gate_pre)
    gate_act = gate_pre * gate_sig
    gated = mixed * gate_act
    d_normed_y = contract(cot_all, full_out, 1, 0)
    scaled = d_normed_y * gate_gain
    width_all = 4 * wide
    sums = sum_tn(jnp.stack([jnp.sum(gated * gated, axis=1), jnp.sum(gated * scaled, axis=1)]))
    gate_rms = lax.rsqrt(sums[0] / width_all + EPS)[:, None]
    inner = sums[1][:, None]
    normed_y = (gated * gate_rms * gate_gain).astype(BF)
    grad_gate_part = jnp.sum(d_normed_y * gated * gate_rms, axis=0)
    d_gated = gate_rms * scaled - gated * (gate_rms * gate_rms * gate_rms) * inner / width_all
    gate_low = (d_gated * mixed * (gate_sig * (1 + gate_pre * (1 - gate_sig)))).astype(BF)

    grad_z_full = contract(normed, gate_low, 0, 0)
    grad_out_full = contract(cot_all, normed_y, 0, 0)
    early = scatter_dp(jnp.concatenate([grad_z_full, grad_out_full], axis=1).astype(BF))
    grad_w_z = early[:, :wide]
    grad_w_out = early[:, wide:].T

    partial_out = contract(normed_y, full_out, 1, 1)
    output = (resid + scatter_tn(partial_out)).astype(BF)

    d_x, d_bc_part, d_dt, grad_conv_x_part, grad_conv_bc_part, grad_head_part = mixer_back(
        d_gated * gate_act
    )
    x_low = d_x.astype(BF)
    dt_low = d_dt.astype(BF)
    bc_part = d_bc_part.astype(BF)
    by_quarter = d_bc_part.reshape(-1, 4, quarter).transpose(1, 0, 2)
    bc_low = scatter_tn(by_quarter.reshape(-1, quarter)).astype(BF)

    late_low = jnp.concatenate([x_low, bc_low, dt_low], axis=1)
    grad_late = contract(normed, late_low, 0, 0)
    gain_part = jnp.sum(grad_z_full * full_z.astype(F32), axis=1) + jnp.sum(
        grad_late[:, :wide] * full_x.astype(F32), axis=1
    )
    own_bc = lax.dynamic_slice_in_dim(full_bc, rank * quarter, quarter, 1)
    gain_part = gain_part + jnp.sum(grad_late[:, wide : wide + quarter] * own_bc, axis=1)
    gain_part = gain_part + jnp.sum(grad_late[:, wide + quarter :] * full_dt, axis=1)
    gain_part = gain_part / norm_gain
    vector = jnp.concatenate(
        [
            gain_part,
            grad_conv_bc_part.reshape(-1),
            grad_conv_x_part.reshape(-1),
            grad_head_part.reshape(-1),
            grad_gate_part,
        ]
    )
    block = w_x.shape[0]
    columns = -(-vector.shape[0] // block)
    vector = jnp.pad(vector, (0, columns * block - vector.shape[0])).reshape(1, block, columns)
    count = lax.axis_size(DP)
    vector = jnp.broadcast_to(vector, (count, block, columns)).reshape(count * block, columns)
    late = scatter_dp(jnp.concatenate([grad_late, vector], axis=1).astype(BF))
    grad_w_x = late[:, :wide]
    bc_own = late[:, wide : wide + quarter]
    grad_w_dt = late[:, wide + quarter : wide + quarter + heads]
    vector = late[:, wide + quarter + heads :].reshape(-1)
    sizes = [norm_gain.size, conv_bc.size, conv_x.size, head_params.size, gate_gain.size]
    starts = [sum(sizes[:i]) for i in range(len(sizes) + 1)]
    shared = sum_tn(vector[: starts[2]])
    grad_norm_gain = shared[: starts[1]]
    grad_conv_bc = shared[starts[1] :].reshape(conv_bc.shape)
    grad_conv_x = vector[starts[2] : starts[3]].reshape(conv_x.shape)
    grad_head = vector[starts[3] : starts[4]].reshape(head_params.shape)
    grad_gate_gain = vector[starts[4] : starts[5]]
    parts = [bc_own] + [
        lax.ppermute(bc_own, TN, [(i, i ^ mask) for i in range(4)]) for mask in (1, 2, 3)
    ]
    stacked = jnp.stack(parts)
    order = jnp.arange(4) ^ rank
    grad_w_bc = jnp.take(stacked, order, axis=0).transpose(1, 0, 2).reshape(block, states)

    partial_in = contract(gate_low, full_z, 1, 1) + contract(
        late_low, jnp.concatenate([full_x, own_bc, full_dt], axis=1), 1, 1
    )
    d_normed = scatter_tn(partial_in)
    d_scaled = d_normed * norm_gain
    cubed = inv_rms * inv_rms * inv_rms
    input_grad = (
        inv_rms * d_scaled
        - resid * cubed * jnp.sum(resid * d_scaled, axis=1, keepdims=True) / resid.shape[1]
        + cotangent.astype(F32)
    )
    return (
        output,
        input_grad,
        grad_norm_gain,
        grad_w_z,
        grad_w_x,
        grad_w_bc,
        grad_w_dt,
        grad_conv_x,
        grad_conv_bc,
        grad_head,
        grad_gate_gain,
        grad_w_out,
    )


def solution(mesh):
    fine = Mesh(mesh.devices.reshape(2, 4, 4, 2, 2), AXES)
    placed = (
        P(AXES, None),
        P(AXES, None),
        P(),
        P(DP, TN),
        P(DP, TN),
        P(DP, None),
        P(DP, TN),
        P(None, TN),
        P(),
        P(None, TN),
        P(TN),
        P(TN, DP),
    )
    return jax.shard_map(
        on_device,
        mesh=fine,
        in_specs=placed,
        out_specs=(
            P(AXES, None),
            P(AXES, None),
            P(),
            P(DP, TN),
            P(DP, TN),
            P(DP, None),
            P(DP, TN),
            P(None, TN),
            P(),
            P(None, TN),
            P(TN),
            P(TN, DP),
        ),
        check_vma=False,
    )
```

time: 1940 us -> 782 us (0.40)
  waiting for transfers between devices: 953 us -> 156 us
  blocking collectives: 467 us -> 0 us
  starting transfers between devices: 0.65 us -> 64.1 us
  local copies, waits for them, and re-layouts: 241 us -> 281 us
  other arithmetic: 69.5 us -> 106 us
    reduce_scatter x6 -> x0, waiting for transfers between devices: 951 us -> none  [the longest x1 232 us: on_device(): lax.psum_scatter(grad_z_full, 'dp', scatter_dimension=0, tiled=True)]
    psum x5 -> x0, blocking collectives: 299 us -> none  [the longest x1 151 us: on_device(): lax.psum((grad_conv_x_part, grad_head_part, grad_gate_part, grad_conv_bc_...]
    all_gather x2 -> x0, blocking collectives: 168 us -> none  [the longest x1 84.3 us: fetch_inputs(): lax.all_gather(w_bc, 'dp', axis=0, tiled=True)]
    ppermute x0 -> x19, waiting for transfers between devices: none -> 120 us  [the longest x10 118 us: swap(): return lax.ppermute(value, axis, [(0, 1), (1, 0)])]
    all_to_all x0 -> x4, starting transfers between devices: none -> 41.6 us  [the longest x2 22.4 us: gather_dp(): got = lax.all_to_all(spread, DP, 0, 0, tiled=True)]
    all_to_all x0 -> x4, waiting for transfers between devices: none -> 35.8 us  [the longest x2 20.6 us: gather_dp(): got = lax.all_to_all(spread, DP, 0, 0, tiled=True)]
    ppermute x0 -> x19, starting transfers between devices: none -> 22.4 us  [the longest x10 12.2 us: swap(): return lax.ppermute(value, axis, [(0, 1), (1, 0)])]
    dot_general x9 -> x7, matrix products: 42.6 us -> 37.2 us  [contract(): lax.dot_general(left, right, (((left_dim,), (right_dim,)), ((), ())), pre...]
  transfers between devices with their start and end apart: 12 -> 23, of which waited for: 5 -> 8; matrix products, arithmetic and copies ran while one was open for 13% -> 33% of each run, Pallas kernels for 0% -> 0%
where the time goes in v1:
time: 782 us; the launch traced here: 769 us
  local copies, waits for them, and re-layouts  281 us (36%)
  matrix products  158 us (20%)
  waiting for transfers between devices  156 us (20%)
  other arithmetic  106 us (14%)
  starting transfers between devices  64.1 us (8%)
    dynamic_update_slice x24, local copies, waits for them, and re-layouts, state_scan(): lax.scan(jax.checkpoint(one_block), initial, (x_blocks, dt_blocks, b_bloc...  155 us
    ppermute x10, waiting for transfers between devices, swap(): return lax.ppermute(value, axis, [(0, 1), (1, 0)])  118 us
    dot_general x12, matrix products, one_block(): jnp.einsum('ijh,jhp->ihp', weights, x_part, precision=lax.Precision.HIGHEST)  51.8 us
    dot_general x7, matrix products, contract(): lax.dot_general(left, right, (((left_dim,), (right_dim,)), ((), ())), pre...  37.2 us
    unnamed x176, local copies, waits for them, and re-layouts  29 us
    another operation x49, other arithmetic  23.8 us
    all_to_all x2, starting transfers between devices, gather_dp(): got = lax.all_to_all(spread, DP, 0, 0, tiled=True)  22.4 us
    all_to_all x2, waiting for transfers between devices, gather_dp(): got = lax.all_to_all(spread, DP, 0, 0, tiled=True)  20.6 us
  transfers between devices with their start and end apart: 23, of which 8 were waited for; matrix products, arithmetic and copies ran while one was open for 33% of the time, Pallas kernels for 0%

profile of v1, /device:TPU:1, one launch (start us, length us, event | category | flops | bytes accessed | tf_op | source)
XLA Modules:
  0.0 768.6 jit_solution(16684500312459358955)
XLA Ops:
  3.6 16.1 %collective-permute-done.2 = bf16[256,1536]{1,0:T(8,128)(2,1)S(1)} collective-permute-done((bf16[256,1536]{1,0:T(8,128)(2,1)}, bf16[256,1536]{1,0:T(8,128)(2,1)S(1)}, u32[]{:S(2)}, u32[]{:S(2)}) %collective-permute-start.2) | collective-permute-done | bytes 786464 | tf_op jit(solution)/shard_map/ppermute | solution.py:88
  19.7 16.9 %collective-permute-done = bf16[256,1536]{1,0:T(8,128)(2,1)S(1)} collective-permute-done((bf16[256,1536]{1,0:T(8,128)(2,1)}, bf16[256,1536]{1,0:T(8,128)(2,1)S(1)}, u32[]{:S(2)}, u32[]{:S(2)}) %collective-permute-start) | collective-permute-done | bytes 786464 | tf_op jit(solution)/shard_map/ppermute | solution.py:88
  45.4 10.9 %all-to-all-start = ((bf16[32,48,1036]{2,1,0:T(8,128)(2,1)}), bf16[32,48,1036]{2,1,0:T(8,128)(2,1)S(1)}, u32[]{:S(2)}, u32[]{:S(2)}) async-start(bf16[32,48,1036]{2,1,0:T(8,128)(2,1)} %broadcast_in_dim.205), calls=%async_computation | async-start | bytes 7077888 | tf_op jit(solution)/shard_map/all_to_all | solution.py:94
  71.3 4.6 copy.240
  80.7 20.6 %all-to-all-done = bf16[32,48,1036]{2,1,0:T(8,128)(2,1)S(1)} async-done(((bf16[32,48,1036]{2,1,0:T(8,128)(2,1)}), bf16[32,48,1036]{2,1,0:T(8,128)(2,1)S(1)}, u32[]{:S(2)}, u32[]{:S(2)}) %all-to-all-start) | async-done | bytes 3182624 | tf_op jit(solution)/shard_map/all_to_all | solution.py:94
  101.2 3.7 broadcast_in_dim.207
  104.9 11.5 %all-to-all-start.1 = ((bf16[32,48,1536]{2,1,0:T(8,128)(2,1)}), bf16[32,48,1536]{2,1,0:T(8,128)(2,1)}, u32[]{:S(2)}, u32[]{:S(2)}) async-start(bf16[32,48,1536]{2,1,0:T(8,128)(2,1)} %broadcast_in_dim.207), calls=%async_computation.1 | async-start | bytes 9437184 | tf_op jit(solution)/shard_map/all_to_all | solution.py:94
  117.3 4.0 fusion.151
  121.3 4.3 fusion.153
  128.8 4.3 fusion.132
  134.2 3.7 fusion.103
  140.3 3.0 reshape.447
  143.3 4.1 copy.222
  149.7 126.3 %while.44 = (s32[]{:T(128)}, f32[12,128,64]{1,2,0:T(8,128)S(1)}, f32[4,256,12,64]{1,0,3,2:T(4,128)}, f32[4,12,128,64]{2,3,1,0:T(8,128)}, f32[4,256,12]{1,2,0:T(8...) while((s32[]{:T(128)}, f32[12,128,64]{1,2,0:T(8,128)S(1)}, ...), condition=%wide.region_4.5_spmd.clone.clone, body=%wide.region_1.0_spmd.clone.clone.sunk | while | flops 1313842176 | bytes 10902735 | solution.py:58
  157.7 5.0 fusion.267
  163.6 17.9 %dynamic_update_slice.74 = f32[4,256,12,64]{1,0,3,2:T(4,128)} dynamic-update-slice(f32[4,256,12,64]{1,0,3,2:T(4,128)} %get-tuple-element.1159, f32[1,256,12,64]{1,0,3,2:T(1,128)S(1)} %copy.345, s32[]{:T(128)S(6)} %copy.356, s32[]{:T(128)} %constant.183.clone.1..sunk.1, s32[]{:T(128)} %constant.183.clone.1..sunk.1, s32[]{:T(128)} %constant.183.clone.1..sunk.1) | dynamic-update-slice | bytes 1572868 | tf_op jit(solution)/shard_map/jvp()/while/body/jit(dynamic_update_index_in_dim)/dynamic_update_slice | solution.py:58
  189.3 5.0 fusion.267
  195.1 17.9 %dynamic_update_slice.74 = f32[4,256,12,64]{1,0,3,2:T(4,128)} dynamic-update-slice(f32[4,256,12,64]{1,0,3,2:T(4,128)} %get-tuple-element.1159, f32[1,256,12,64]{1,0,3,2:T(1,128)S(1)} %copy.345, s32[]{:T(128)S(6)} %copy.356, s32[]{:T(128)} %constant.183.clone.1..sunk.1, s32[]{:T(128)} %constant.183.clone.1..sunk.1, s32[]{:T(128)} %constant.183.clone.1..sunk.1) | dynamic-update-slice | bytes 1572868 | tf_op jit(solution)/shard_map/jvp()/while/body/jit(dynamic_update_index_in_dim)/dynamic_update_slice | solution.py:58
  220.8 5.0 fusion.267
  226.6 17.9 %dynamic_update_slice.74 = f32[4,256,12,64]{1,0,3,2:T(4,128)} dynamic-update-slice(f32[4,256,12,64]{1,0,3,2:T(4,128)} %get-tuple-element.1159, f32[1,256,12,64]{1,0,3,2:T(1,128)S(1)} %copy.345, s32[]{:T(128)S(6)} %copy.356, s32[]{:T(128)} %constant.183.clone.1..sunk.1, s32[]{:T(128)} %constant.183.clone.1..sunk.1, s32[]{:T(128)} %constant.183.clone.1..sunk.1) | dynamic-update-slice | bytes 1572868 | tf_op jit(solution)/shard_map/jvp()/while/body/jit(dynamic_update_index_in_dim)/dynamic_update_slice | solution.py:58
  252.3 5.0 fusion.267
  258.1 17.9 %dynamic_update_slice.74 = f32[4,256,12,64]{1,0,3,2:T(4,128)} dynamic-update-slice(f32[4,256,12,64]{1,0,3,2:T(4,128)} %get-tuple-element.1159, f32[1,256,12,64]{1,0,3,2:T(1,128)S(1)} %copy.345, s32[]{:T(128)S(6)} %copy.356, s32[]{:T(128)} %constant.183.clone.1..sunk.1, s32[]{:T(128)} %constant.183.clone.1..sunk.1, s32[]{:T(128)} %constant.183.clone.1..sunk.1) | dynamic-update-slice | bytes 1572868 | tf_op jit(solution)/shard_map/jvp()/while/body/jit(dynamic_update_index_in_dim)/dynamic_update_slice | solution.py:58
  281.0 5.4 fusion.115
  286.4 8.6 %multiply_reduce_fusion.13 = (f32[1024]{0:T(1024)S(1)}, f32[1024]{0:T(1024)S(1)}, f32[1024,768]{1,0:T(8,128)}, f32[1024,768]{1,0:T(8,128)}) fusion(f32[768]{0:T(1024)S(1)} %copy-done.75, f32[1024,768]{1,0:T(8,128)S(1)} %fusion.115, f32[1024,768]{1,0:T(8,128)S(1)} %copy-done.12, f32[768]{0:T(1024)S(1)} %copy-done.57, f32[1024,768]{1,0:T(8,128)S(1)} %copy-done, ...), kind=kOutput, calls=%fused_computation.163 | convolution fusion | flops 2428499968 | bytes 21248000 | tf_op jit(solution)/shard_map/dot_general | solution.py:82
  295.6 3.2 collective-permute-start.5
  305.1 4.6 copy.251
  310.6 8.4 %multiply_reduce_fusion.7 = (f32[768]{0:T(1024)S(1)}, f32[1024,768]{1,0:T(8,128)}, bf16[1024,768]{1,0:T(8,128)(2,1)}, bf16[768]{0:T(1024)(128)(2,1)}) fusion(f32[1024,768]{1,0:T(8,128)S(1)} %copy-done, f32[1024,768]{1,0:T(8,128)} %copy-done.32, f32[1024]{0:T(1024)S(1)} %bitcast.516, f32[1024,768]{1,0:T(8,128)} %get-tuple-element.864, ...), kind=kLoop, calls=%fused_computation.154 | loop fusion | flops 22804992 | bytes 20470272 | tf_op jit(solution)/shard_map/transpose(jvp())/reduce_sum | solution.py:75
  319.6 8.0 %fusion.162 = (bf16[1536,768]{1,0:T(8,128)(2,1)}, f32[1536]{0:T(1024)}) fusion(bf16[1536,1536]{1,0:T(8,128)(2,1)} %bitcast.17, bf16[1024,1536]{1,0:T(8,128)(2,1)} %fusion.97, bf16[1024,768]{1,0:T(8,128)(2,1)} %get-tuple-element.883), kind=kOutput, calls=%fused_computation.312 | convolution fusion | flops 2420636160 | bytes 9443328 | tf_op jit(solution)/shard_map/dot_general | solution.py:82
  330.0 5.1 reshape.454
  339.7 200.3 %while.43 = (s32[]{:T(128)}, f32[12]{0:T(128)}, f32[12,128,64]{1,2,0:T(8,128)S(1)}, f32[4,256,12,64]{1,0,3,2:T(4,128)}, f32[4,256,12]{1,0,2:T(4,128)}, /*index=5...) while((s32[]{:T(128)}, f32[12]{0:T(128)}, ...), condition=%wide.region_22.23_spmd.clone, body=%wide.region_8.22_spmd.clone.sunk | while | flops 3038789632 | bytes 27654896 | solution.py:58
  342.7 2.7 constant_dynamic-slice_fusion.5
  349.1 5.0 fusion.247
  357.5 2.9 fusion.253
  371.5 17.8 %dynamic_update_slice.71 = f32[4,256,12,64]{1,0,3,2:T(4,128)} dynamic-update-slice(f32[4,256,12,64]{1,0,3,2:T(4,128)} %get-tuple-element.1204, f32[1,256,12,64]{1,0,3,2:T(1,128)S(1)} %copy.340, s32[]{:T(128)S(6)} %sub.310, s32[]{:T(128)} %constant.183.clone.1..sunk, s32[]{:T(128)} %constant.183.clone.1..sunk, s32[]{:T(128)} %constant.183.clone.1..sunk) | dynamic-update-slice | bytes 1572868 | tf_op jit(solution)/shard_map/transpose(jvp())/while/body/jit(dynamic_update_index_in_dim)/dynamic_update_slice | solution.py:58
  398.6 5.0 fusion.247
  406.9 2.9 fusion.253
  421.6 17.8 %dynamic_update_slice.71 = f32[4,256,12,64]{1,0,3,2:T(4,128)} dynamic-update-slice(f32[4,256,12,64]{1,0,3,2:T(4,128)} %get-tuple-element.1204, f32[1,256,12,64]{1,0,3,2:T(1,128)S(1)} %copy.340, s32[]{:T(128)S(6)} %sub.310, s32[]{:T(128)} %constant.183.clone.1..sunk, s32[]{:T(128)} %constant.183.clone.1..sunk, s32[]{:T(128)} %constant.183.clone.1..sunk) | dynamic-update-slice | bytes 1572868 | tf_op jit(solution)/shard_map/transpose(jvp())/while/body/jit(dynamic_update_index_in_dim)/dynamic_update_slice | solution.py:58
  448.7 5.0 fusion.247
  457.0 2.9 fusion.253
  471.7 17.8 %dynamic_update_slice.71 = f32[4,256,12,64]{1,0,3,2:T(4,128)} dynamic-update-slice(f32[4,256,12,64]{1,0,3,2:T(4,128)} %get-tuple-element.1204, f32[1,256,12,64]{1,0,3,2:T(1,128)S(1)} %copy.340, s32[]{:T(128)S(6)} %sub.310, s32[]{:T(128)} %constant.183.clone.1..sunk, s32[]{:T(128)} %constant.183.clone.1..sunk, s32[]{:T(128)} %constant.183.clone.1..sunk) | dynamic-update-slice | bytes 1572868 | tf_op jit(solution)/shard_map/transpose(jvp())/while/body/jit(dynamic_update_index_in_dim)/dynamic_update_slice | solution.py:58
  498.8 5.0 fusion.247
  507.1 2.9 fusion.253
  521.8 17.8 %dynamic_update_slice.71 = f32[4,256,12,64]{1,0,3,2:T(4,128)} dynamic-update-slice(f32[4,256,12,64]{1,0,3,2:T(4,128)} %get-tuple-element.1204, f32[1,256,12,64]{1,0,3,2:T(1,128)S(1)} %copy.340, s32[]{:T(128)S(6)} %sub.310, s32[]{:T(128)} %constant.183.clone.1..sunk, s32[]{:T(128)} %constant.183.clone.1..sunk, s32[]{:T(128)} %constant.183.clone.1..sunk) | dynamic-update-slice | bytes 1572868 | tf_op jit(solution)/shard_map/transpose(jvp())/while/body/jit(dynamic_update_index_in_dim)/dynamic_update_slice | solution.py:58
  541.5 4.3 copy.313
  545.8 3.7 copy.232
  549.5 10.0 %multiply_reduce_fusion.11 = (f32[768]{0:T(1024)S(1)}, f32[768]{0:T(1024)S(1)}, f32[768]{0:T(1024)S(1)}, f32[768]{0:T(1024)S(1)}, f32[768]{0:T(1024)S(1)}, /*index=5*/f32[1024,768]{1,0:T(8,128)}) fusion(f32[1024,768]{1,0:T(8,128)} %fusion.153, f32[1024,768]{1,0:T(8,128)S(1)} %copy-done.1, f32[1024,768]{1,0:T(8,128)} %copy.232, ...), kind=kLoop, calls=%fused_computation.158 | loop fusion | flops 15724800 | bytes 15747072 | tf_op jit(solution)/shard_map/transpose(jvp())/reduce_sum | solution.py:21
  562.9 5.7 broadcast_multiply_fusion
  577.6 4.0 fusion.101
  584.1 4.4 fusion.166
  589.7 3.3 copy.239
  595.4 10.4 %all-to-all-start.2 = ((bf16[32,48,1000]{2,1,0:T(8,128)(2,1)}), bf16[32,48,1000]{2,1,0:T(8,128)(2,1)S(1)}, u32[]{:S(2)}, u32[]{:S(2)}) async-start(bf16[32,48,1000]{2,1,0:T(8,128)(2,1)} %pad_maximum_fusion.2), calls=%async_computation.2 | async-start | bytes 6291456 | tf_op jit(solution)/shard_map/all_to_all | solution.py:100
  605.8 5.4 fusion.110
  611.3 3.4 fusion.104
  614.7 4.3 convolution_add_fusion.2
  625.2 3.1 convolution_convert_fusion
  628.4 2.8 pad_maximum_fusion
  631.2 15.2 %all-to-all-done.2 = bf16[32,48,1000]{2,1,0:T(8,128)(2,1)S(1)} async-done(((bf16[32,48,1000]{2,1,0:T(8,128)(2,1)}), bf16[32,48,1000]{2,1,0:T(8,128)(2,1)S(1)}, u32[]{:S(2)}, u32[]{:S(2)}) %all-to-all-start.2) | async-done | bytes 3072032 | tf_op jit(solution)/shard_map/all_to_all | solution.py:100
  646.4 8.9 %all-to-all-start.3 = ((bf16[32,48,1536]{2,1,0:T(8,128)(2,1)}), bf16[32,48,1536]{2,1,0:T(8,128)(2,1)}, u32[]{:S(2)}, u32[]{:S(2)}) async-start(bf16[32,48,1536]{2,1,0:T(8,128)(2,1)} %pad_maximum_fusion), calls=%async_computation.3 | async-start | bytes 9437184 | tf_op jit(solution)/shard_map/all_to_all | solution.py:100
  655.3 2.9 bitcast_add_fusion
  658.3 3.3 collective-permute-start.12
  661.6 2.9 bitcast_add_fusion.1
  664.8 66.1 %collective-permute-done.12 = bf16[256,1536]{1,0:T(8,128)(2,1)S(1)} collective-permute-done((bf16[256,1536]{1,0:T(8,128)(2,1)S(1)}, bf16[256,1536]{1,0:T(8,128)(2,1)S(1)}, u32[]{:S(2)}, u32[]{:S(2)}) %collective-permute-start.12) | collective-permute-done | bytes 786464 | tf_op jit(solution)/shard_map/ppermute | solution.py:88
  731.3 16.4 %collective-permute-done.8 = bf16[256,1536]{1,0:T(8,128)(2,1)S(1)} collective-permute-done((bf16[256,1536]{1,0:T(8,128)(2,1)S(1)}, bf16[256,1536]{1,0:T(8,128)(2,1)S(1)}, u32[]{:S(2)}, u32[]{:S(2)}) %collective-permute-start.8) | collective-permute-done | bytes 786464 | tf_op jit(solution)/shard_map/ppermute | solution.py:88
  764.6 3.0 convert_reduce_fusion
  (586 shorter events, 233.4 us)
Async XLA Ops:
  0.6 19.1 %collective-permute-start.2 = (bf16[256,1536]{1,0:T(8,128)(2,1)}, bf16[256,1536]{1,0:T(8,128)(2,1)S(1)}, u32[]{:S(2)}, u32[]{:S(2)}) collective-permute-start(bf16[256,1536]{1,0:T(8,128)(2,1)} %param.17), channel_id=1, source_target_pairs={{0,2},{2,0},{1,3},{3,1},{4,6},{6,4},{5,7},{7,5},{8,10},{10,8},{9,1... | collective-permute-start | bytes 2359304 | tf_op jit(solution)/shard_map/ppermute | solution.py:88
  2.8 33.8 %collective-permute-start = (bf16[256,1536]{1,0:T(8,128)(2,1)}, bf16[256,1536]{1,0:T(8,128)(2,1)S(1)}, u32[]{:S(2)}, u32[]{:S(2)}) collective-permute-start(bf16[256,1536]{1,0:T(8,128)(2,1)} %param.16), channel_id=1, source_target_pairs={{0,2},{2,0},{1,3},{3,1},{4,6},{6,4},{5,7},{7,5},{8,10},{10,8},{9,1... | collective-permute-start | bytes 2359304 | tf_op jit(solution)/shard_map/ppermute | solution.py:88
  41.6 23.1 %collective-permute-start.1 = (bf16[2,256,1536]{2,1,0:T(8,128)(2,1)}, bf16[2,256,1536]{2,1,0:T(8,128)(2,1)}, u32[]{:S(2)}, u32[]{:S(2)}) collective-permute-start(bf16[2,256,1536]{2,1,0:T(8,128)(2,1)} %pad_maximum_fusion.4), channel_id=1, source_target_pairs={{0,1},{1,0},{2,3},{3,2},{4,5},{5,4},{6,7},{7,6},{8,9},{9,8},{10,11... | collective-permute-start | bytes 4718600 | tf_op jit(solution)/shard_map/ppermute | solution.py:88
  45.4 11.0 %copy-start.79 = (f32[3,12]{1,0:T(4,128)S(1)}, f32[3,12]{1,0:T(4,128)}, u32[]{:S(2)}) copy-start(f32[3,12]{1,0:T(4,128)} %param.25) | copy-start | bytes 436
  45.4 55.8 %all-to-all-start = ((bf16[32,48,1036]{2,1,0:T(8,128)(2,1)}), bf16[32,48,1036]{2,1,0:T(8,128)(2,1)S(1)}, u32[]{:S(2)}, u32[]{:S(2)}) async-start(bf16[32,48,1036]{2,1,0:T(8,128)(2,1)} %broadcast_in_dim.205), calls=%async_computation | async-start | bytes 7077888 | tf_op jit(solution)/shard_map/all_to_all | solution.py:94
  57.7 6.3 copy-start.50
  57.7 6.3 copy-start.51
  57.7 7.0 copy-start.21
  57.7 7.0 copy-start.23
  61.5 6.2 collective-permute-start.3
  101.2 24.4 %copy-start.3 = (bf16[32,48,1036]{2,1,0:T(8,128)(2,1)}, bf16[32,48,1036]{2,1,0:T(8,128)(2,1)S(1)}, u32[]{:S(2)}) copy-start(bf16[32,48,1036]{2,1,0:T(8,128)(2,1)S(1)} %all-to-all-done) | copy-start | bytes 9547780
  104.9 176.0 %all-to-all-start.1 = ((bf16[32,48,1536]{2,1,0:T(8,128)(2,1)}), bf16[32,48,1536]{2,1,0:T(8,128)(2,1)}, u32[]{:S(2)}, u32[]{:S(2)}) async-start(bf16[32,48,1536]{2,1,0:T(8,128)(2,1)} %broadcast_in_dim.207), calls=%async_computation.1 | async-start | bytes 9437184 | tf_op jit(solution)/shard_map/all_to_all | solution.py:94
  127.2 7.1 copy-start.11
  127.2 7.1 copy-start.53
  127.2 7.1 copy-start.64
  281.0 5.4 copy-start.12
  281.0 5.4 copy-start.57
  281.0 5.4 copy-start.75
  286.4 8.7 %copy-start.32 = (f32[1024,768]{1,0:T(8,128)}, f32[1024,768]{1,0:T(8,128)S(1)}, u32[]{:S(2)}) copy-start(f32[1024,768]{1,0:T(8,128)S(1)} %fusion.115) | copy-start | bytes 9437188
  286.4 13.4 %copy-start.36 = (bf16[1536,256]{1,0:T(8,128)(2,1)S(1)}, bf16[1536,256]{1,0:T(8,128)(2,1)}, u32[]{:S(2)}) copy-start(bf16[1536,256]{1,0:T(8,128)(2,1)} %slice.271) | copy-start | bytes 2359300
  286.4 14.3 %copy-start.4 = (bf16[32,48,1036]{2,1,0:T(8,128)(2,1)S(1)}, bf16[32,48,1036]{2,1,0:T(8,128)(2,1)}, u32[]{:S(2)}) copy-start(bf16[32,48,1036]{2,1,0:T(8,128)(2,1)} %copy-done.3) | copy-start | bytes 9547780
  295.6 14.1 %collective-permute-start.5 = (f32[2,1024]{1,0:T(2,128)}, f32[2,1024]{1,0:T(2,128)}, u32[]{:S(2)}, u32[]{:S(2)}) collective-permute-start(f32[2,1024]{1,0:T(2,128)} %pad_maximum_fusion.11), channel_id=1, source_target_pairs={{0,2},{1,3},{2,0},{3,1},{4,6},{5,7},{6,4},{7,5},{8,10},{9,11},{10,... | collective-permute-start | bytes 24584 | tf_op jit(solution)/shard_map/ppermute | solution.py:117
  298.8 10.9 %collective-permute-start.6 = (f32[2,1024]{1,0:T(2,128)}, f32[2,1024]{1,0:T(2,128)}, u32[]{:S(2)}, u32[]{:S(2)}) collective-permute-start(f32[2,1024]{1,0:T(2,128)} %pad_maximum_fusion.11), channel_id=1, source_target_pairs={{0,3},{1,2},{2,1},{3,0},{4,7},{5,6},{6,5},{7,4},{8,11},{9,10},{10,... | collective-permute-start | bytes 24584 | tf_op jit(solution)/shard_map/ppermute | solution.py:117
  299.5 10.3 %collective-permute-start.4 = (f32[2,1024]{1,0:T(2,128)}, f32[2,1024]{1,0:T(2,128)}, u32[]{:S(2)}, u32[]{:S(2)}) collective-permute-start(f32[2,1024]{1,0:T(2,128)} %pad_maximum_fusion.11), channel_id=1, source_target_pairs={{0,1},{1,0},{2,3},{3,2},{4,5},{5,4},{6,7},{7,6},{8,9},{9,8},{10,11... | collective-permute-start | bytes 24584 | tf_op jit(solution)/shard_map/ppermute | solution.py:117
  303.2 6.6 copy-start.66
  303.2 6.6 copy-start.68
  303.2 7.4 copy-start.58
  303.2 7.4 copy-start.76
  310.5 8.4 %copy-start.55 = (f32[1,1024]{1,0:T(1,128)}, f32[1,1024]{1,0:T(1,128)S(1)}, u32[]{:S(2)}) copy-start(f32[1,1024]{1,0:T(1,128)S(1)} %get-tuple-element.912) | copy-start | bytes 12292
  319.6 8.0 %copy-start.2 = (f32[1024,768]{1,0:T(8,128)S(1)}, f32[1024,768]{1,0:T(8,128)}, u32[]{:S(2)}) copy-start(f32[1024,768]{1,0:T(8,128)} %get-tuple-element.859) | copy-start | bytes 9437188
  549.5 10.1 %copy-start.24 = (f32[1024,256]{1,0:T(8,128)S(1)}, f32[1024,256]{1,0:T(8,128)}, u32[]{:S(2)}) copy-start(f32[1024,256]{1,0:T(8,128)} %fusion.151) | copy-start | bytes 3145732
  549.5 10.1 %copy-start.25 = (f32[1024,256]{1,0:T(8,128)S(1)}, f32[1024,256]{1,0:T(8,128)}, u32[]{:S(2)}) copy-start(f32[1024,256]{1,0:T(8,128)} %get-tuple-element.866) | copy-start | bytes 3145732
  549.5 10.1 %copy-start.34 = (f32[4,256,128]{2,1,0:T(8,128)S(1)}, f32[4,256,128]{2,1,0:T(8,128)}, u32[]{:S(2)}) copy-start(f32[4,256,128]{2,1,0:T(8,128)} %get-tuple-element.445) | copy-start | bytes 1572868
  549.5 10.1 %copy-start.35 = (f32[4,256,128]{2,1,0:T(8,128)S(1)}, f32[4,256,128]{2,1,0:T(8,128)}, u32[]{:S(2)}) copy-start(f32[4,256,128]{2,1,0:T(8,128)} %get-tuple-element.446) | copy-start | bytes 1572868
  562.7 11.5 %collective-permute-start.9 = (bf16[2,1024,64]{2,1,0:T(8,128)(2,1)}, bf16[2,1024,64]{2,1,0:T(8,128)(2,1)}, u32[]{:S(2)}, u32[]{:S(2)}) collective-permute-start(bf16[2,1024,64]{2,1,0:T(8,128)(2,1)} %bitcast.299), channel_id=1, source_target_pairs={{0,1},{1,0},{2,3},{3,2},{4,5},{5,4},{6,7},{7,6},{8,9},{9,8},{10,11... | collective-permute-start | bytes 786440 | tf_op jit(solution)/shard_map/ppermute | solution.py:88
  562.9 5.7 copy-start.60
  562.9 5.8 copy-start.41
  575.8 8.1 %collective-permute-start.10 = (bf16[1024,64]{1,0:T(8,128)(2,1)S(1)}, bf16[1024,64]{1,0:T(8,128)(2,1)S(1)}, u32[]{:S(2)}, u32[]{:S(2)}) collective-permute-start(bf16[1024,64]{1,0:T(8,128)(2,1)S(1)} %fusion.138), channel_id=1, source_target_pairs={{0,2},{2,0},{1,3},{3,1},{4,6},{6,4},{5,7},{7,5},{8,10},{10,8},{9,1... | collective-permute-start | bytes 393224 | tf_op jit(solution)/shard_map/ppermute | solution.py:88
  577.6 6.4 copy-start.8
  577.6 6.4 copy-start.42
  581.6 6.9 copy-start.38
  595.3 10.4 %copy-start.56 = (f32[1,1024]{1,0:T(1,128)S(1)}, f32[1,1024]{1,0:T(1,128)}, u32[]{:S(2)}) copy-start(f32[1,1024]{1,0:T(1,128)} %copy-done.55) | copy-start | bytes 12292
  595.3 10.4 %copy-start.77 = (f32[768]{0:T(1024)S(1)}, f32[768]{0:T(1024)}, u32[]{:S(2)}) copy-start(f32[768]{0:T(1024)} %param.26) | copy-start | bytes 9220
  595.4 51.0 %all-to-all-start.2 = ((bf16[32,48,1000]{2,1,0:T(8,128)(2,1)}), bf16[32,48,1000]{2,1,0:T(8,128)(2,1)S(1)}, u32[]{:S(2)}, u32[]{:S(2)}) async-start(bf16[32,48,1000]{2,1,0:T(8,128)(2,1)} %pad_maximum_fusion.2), calls=%async_computation.2 | async-start | bytes 6291456 | tf_op jit(solution)/shard_map/all_to_all | solution.py:100
  605.8 5.5 copy-start.16
  605.8 5.5 copy-start.39
  605.8 5.5 copy-start.43
  605.8 5.5 copy-start.45
  611.3 10.4 %copy-start.26 = (f32[1024,1536]{1,0:T(8,128)}, f32[1024,1536]{1,0:T(8,128)S(1)}, u32[]{:S(2)}) copy-start(f32[1024,1536]{1,0:T(8,128)S(1)} %fusion.110) | copy-start | bytes 18874372
  619.0 5.9 copy-start.30
  619.0 6.2 copy-start.31
  620.4 34.9 %collective-permute-start.11 = (bf16[2,256,1536]{2,1,0:T(8,128)(2,1)}, bf16[2,256,1536]{2,1,0:T(8,128)(2,1)}, u32[]{:S(2)}, u32[]{:S(2)}) collective-permute-start(bf16[2,256,1536]{2,1,0:T(8,128)(2,1)} %fusion.125), channel_id=1, source_target_pairs={{0,1},{1,0},{2,3},{3,2},{4,5},{5,4},{6,7},{7,6},{8,9},{9,8},{10,11... | collective-permute-start | bytes 4718600 | tf_op jit(solution)/shard_map/ppermute | solution.py:88
  623.8 37.8 %collective-permute-start.7 = (bf16[2,256,1536]{2,1,0:T(8,128)(2,1)}, bf16[2,256,1536]{2,1,0:T(8,128)(2,1)}, u32[]{:S(2)}, u32[]{:S(2)}) collective-permute-start(bf16[2,256,1536]{2,1,0:T(8,128)(2,1)} %fusion.124), channel_id=1, source_target_pairs={{0,1},{1,0},{2,3},{3,2},{4,5},{5,4},{6,7},{7,6},{8,9},{9,8},{10,11... | collective-permute-start | bytes 4718600 | tf_op jit(solution)/shard_map/ppermute | solution.py:88
  646.4 118.2 %all-to-all-start.3 = ((bf16[32,48,1536]{2,1,0:T(8,128)(2,1)}), bf16[32,48,1536]{2,1,0:T(8,128)(2,1)}, u32[]{:S(2)}, u32[]{:S(2)}) async-start(bf16[32,48,1536]{2,1,0:T(8,128)(2,1)} %pad_maximum_fusion), calls=%async_computation.3 | async-start | bytes 9437184 | tf_op jit(solution)/shard_map/all_to_all | solution.py:100
  658.3 72.6 %copy-start.17 = (bf16[256,1536]{1,0:T(8,128)(2,1)S(1)}, bf16[256,1536]{1,0:T(8,128)(2,1)}, u32[]{:S(2)}) copy-start(bf16[256,1536]{1,0:T(8,128)(2,1)} %param.16) | copy-start | bytes 2359300
  658.3 72.5 %collective-permute-start.12 = (bf16[256,1536]{1,0:T(8,128)(2,1)S(1)}, bf16[256,1536]{1,0:T(8,128)(2,1)S(1)}, u32[]{:S(2)}, u32[]{:S(2)}) collective-permute-start(bf16[256,1536]{1,0:T(8,128)(2,1)S(1)} %fusion.134), channel_id=1, source_target_pairs={{0,2},{2,0},{1,3},{3,1},{4,6},{6,4},{5,7},{7,5},{8,10},{10,8},{9,1... | collective-permute-start | bytes 2359304 | tf_op jit(solution)/shard_map/ppermute | solution.py:88
  664.5 83.2 %copy-start.29 = (bf16[256,1536]{1,0:T(8,128)(2,1)S(1)}, bf16[256,1536]{1,0:T(8,128)(2,1)}, u32[]{:S(2)}) copy-start(bf16[256,1536]{1,0:T(8,128)(2,1)} %param.17) | copy-start | bytes 2359300
  664.6 83.1 %collective-permute-start.8 = (bf16[256,1536]{1,0:T(8,128)(2,1)S(1)}, bf16[256,1536]{1,0:T(8,128)(2,1)S(1)}, u32[]{:S(2)}, u32[]{:S(2)}) collective-permute-start(bf16[256,1536]{1,0:T(8,128)(2,1)S(1)} %fusion.133), channel_id=1, source_target_pairs={{0,2},{2,0},{1,3},{3,1},{4,6},{6,4},{5,7},{7,5},{8,10},{10,8},{9,1... | collective-permute-start | bytes 2359304 | tf_op jit(solution)/shard_map/ppermute | solution.py:88
  750.5 9.4 %collective-permute-start.14 = (f32[2816]{0:T(1024)S(1)}, f32[2816]{0:T(1024)S(1)}, u32[]{:S(2)}, u32[]{:S(2)}) collective-permute-start(f32[2816]{0:T(1024)S(1)} %slice.282), channel_id=1, source_target_pairs={{0,2},{1,3},{2,0},{3,1},{4,6},{5,7},{6,4},{7,5},{8,10},{9,11},{10,... | collective-permute-start | bytes 33800 | tf_op jit(solution)/shard_map/ppermute | solution.py:117
  752.8 7.1 collective-permute-start.15
  754.1 5.8 collective-permute-start.13
  755.9 5.3 collective-permute-start.17
  757.2 4.0 collective-permute-start.16
  759.9 3.3 collective-permute-start.18
  (39 other events, 111.7 us)
